TPU v7x, 32 devices: a whole 2x2x4 slice. The times are simulated.
32 devices in a mesh: seq: 16 (over z, y, x), head: 2 (over core).
Axes of the slice: x: 2, y: 2, z: 4, core: 2. Of those that a mesh axis runs over, the one named last changes fastest.
Arguments:
- hidden: bfloat16 [2048, 2048], P('seq'), may hold values from -6 to 6
- queries: bfloat16 [2048, 3072], P('seq', 'head'), may hold values from -90 to 90
- req_len: int32 [2], replicated, may hold values from 1 to 1920, 2048 in all
- req_offset: int32 [2], replicated, may hold values from 0 to 4095
- expert_ids: int32 [2048, 6], P('seq'), may hold values from 0 to 15, all different within a row; in each aligned block of 128 rows (0 to 127, 128 to 255, ...) at most 64 rows name the same one
- decode_slot: int32 [128], replicated, may hold values from 0 to 127, as said below
- attn_gain: float32 [2048], replicated, may hold values from 0.25 to 1.75
- kv_down: bfloat16 [2048, 576], replicated, may hold values from -0.125 to 0.125
- kv_gain: float32 [512], replicated, may hold values from 0.25 to 1.75
- key_up: bfloat16 [16, 128, 512], P('head'), may hold values from -0.5 to 0.5
- value_up: bfloat16 [16, 512, 128], P('head'), may hold values from -0.25 to 0.25
- out_proj: bfloat16 [2048, 2048], P('head'), may hold values from -0.5 to 0.5
- ffn_gain: float32 [2048], replicated, may hold values from 0.25 to 1.75
- router: float32 [2048, 16], replicated, may hold values from -0.125 to 0.125
- expert_gate_up: bfloat16 [16, 2, 2048, 1408], P('seq', None, None, 'head'), may hold values from -0.125 to 0.125
- expert_down: bfloat16 [16, 1408, 2048], P('seq', 'head'), may hold values from -0.15625 to 0.15625
Outputs:
- output: bfloat16 [2048, 2048], P('seq', 'head')
- decode_latent: bfloat16 [128, 16, 512], P(('seq', 'head'))
- decode_rope: bfloat16 [128, 1024], P(('seq', 'head'))
Inputs may be any that keep to these rules, and one draw needn't show every extreme that they name: `req_len`: the lengths sum to 2048. `expert_ids`: the 128 rows of one index of seq name one expert at most 64 times in all. `decode_slot`: all entries differ; slot g belongs to device g // 4 in the order seq then head, and all 4 slots of some device are named.
All inputs are finite; a program needn't handle non-finite values.
Results may differ from a plain program's by a relative error of at most 0.02.
Values may be sent and summed in bfloat16 or wider, within the bound.
A program may use at most 128 MiB of HBM per device.

v0:
```python
import math

import jax
import jax.numpy as jnp
from jax import lax
from jax.sharding import PartitionSpec as P

D = 2048
NOPE = 128
ROPE = 64
V_HEAD = 128
KV_RANK = 512
TOP = 6
BLOCK = 16
DEC_SLOTS = 4


ROPE_BASE = 50000.0
ROUTE_SCALE = 2.446
EPSILON = 1e-06
MASKED = -1e30


def rms_rows(values, scale_gain):
    values = values.astype(jnp.float32)
    inverse = lax.rsqrt(jnp.mean(values * values, axis=-1, keepdims=True) + EPSILON)
    return values * inverse * scale_gain


def angles(position, rope_width):
    half_width = rope_width // 2
    freq_steps = jnp.arange(half_width).astype(jnp.float32) * (2.0 / rope_width)
    frequency = jnp.exp(-math.log(ROPE_BASE) * freq_steps)
    return position.astype(jnp.float32)[:, None] * frequency[None, :]


def rotate(values, rot_angle):
    half_width = values.shape[-1] // 2
    first_half = values[..., :half_width].astype(jnp.float32)
    second_half = values[..., half_width:].astype(jnp.float32)
    cosine = jnp.cos(rot_angle)
    sine_part = jnp.sin(rot_angle)
    return jnp.concatenate(
        [
            first_half * cosine - second_half * sine_part,
            first_half * sine_part + second_half * cosine,
        ],
        axis=-1,
    )


def request_of(req_len, token_index):
    req_ends = jnp.cumsum(req_len)
    return jnp.sum((token_index[:, None] >= req_ends[None, :]).astype(jnp.int32), axis=1)


def position_of(req_len, req_offset, token_index):
    request = request_of(req_len, token_index)
    req_ends = jnp.cumsum(req_len)
    starts = req_ends - req_len
    member = request[:, None] == jnp.arange(req_len.shape[0])[None, :]
    start_at = jnp.sum(jnp.where(member, starts[None, :], 0), axis=1)
    offset = jnp.sum(jnp.where(member, req_offset[None, :], 0), axis=1)
    return offset + token_index - start_at


def key_width(piece_rows):
    for option_width in (1024, 512, 256, 128):
        return option_width
    return piece_rows


def body(
    hidden,
    queries,
    req_len,
    req_offset,
    expert_ids,
    decode_slot,
    attn_gain,
    kv_down,
    kv_gain,
    key_up,
    value_up,
    out_proj,
    ffn_gain,
    router,
    expert_gate_up,
    expert_down,
):
    head_count = lax.axis_size("head")
    seq_place = lax.axis_index("seq")
    head_place = lax.axis_index("head")
    tok_rows = hidden.shape[0]
    heads_here = key_up.shape[0]
    my_index = seq_place * tok_rows + jnp.arange(tok_rows, dtype=jnp.int32)
    my_request = request_of(req_len, my_index)
    my_turn = angles(position_of(req_len, req_offset, my_index), ROPE)
    normed = rms_rows(hidden, attn_gain).astype(jnp.bfloat16)
    head_view = queries.reshape(tok_rows, heads_here, NOPE + ROPE)
    query_rope = rotate(head_view[:, :, NOPE:], my_turn[:, None, :]).astype(jnp.bfloat16)
    query_latent = jnp.einsum(
        "thn,hnc->thc", head_view[:, :, :NOPE], key_up, preferred_element_type=jnp.float32
    ).astype(jnp.bfloat16)
    query_rows = tok_rows * heads_here
    flat_latent = query_latent.reshape(query_rows, KV_RANK)
    flat_rope = query_rope.reshape(query_rows, ROPE)
    row_token = jnp.repeat(my_index, heads_here)
    row_request = jnp.repeat(my_request, heads_here)
    score_scale = 1.0 / math.sqrt(NOPE + ROPE)
    my_device = seq_place * head_count + head_place
    slot_ids = my_device * DEC_SLOTS + jnp.arange(DEC_SLOTS, dtype=jnp.int32)
    block_ids = jnp.arange(decode_slot.shape[0], dtype=jnp.int32)
    slot_match = decode_slot[None, :] == slot_ids[:, None]
    source_block = jnp.sum(jnp.where(slot_match, block_ids[None, :], 0), axis=1)
    slot_filled = jnp.any(slot_match, axis=1)
    kv_full = jnp.dot(normed, kv_down, preferred_element_type=jnp.float32)
    latent = rms_rows(kv_full[:, :KV_RANK], kv_gain).astype(jnp.bfloat16)
    key_rope = rotate(kv_full[:, KV_RANK:], my_turn).astype(jnp.bfloat16)
    run_peak = jnp.full((query_rows,), MASKED, jnp.float32)
    run_total = jnp.zeros((query_rows,), jnp.float32)
    run_acc = jnp.zeros((query_rows, KV_RANK), jnp.float32)
    piece_latent = lax.all_gather(latent, "seq", axis=0, tiled=True)
    piece_rope = lax.all_gather(key_rope, "seq", axis=0, tiled=True)
    piece_rows = piece_latent.shape[0]
    block_width = key_width(piece_rows)

    def key_block(block_no, loop_state):
        peak_now, total_now, acc_now = loop_state
        offset_rows = block_no * block_width
        block_latent = lax.dynamic_slice_in_dim(piece_latent, offset_rows, block_width, 0)
        block_rope = lax.dynamic_slice_in_dim(piece_rope, offset_rows, block_width, 0)
        key_index = offset_rows + jnp.arange(block_width, dtype=jnp.int32)
        key_request = request_of(req_len, key_index)
        contract = (((1,), (1,)), ((), ()))
        scores = lax.dot_general(
            flat_latent, block_latent, contract, preferred_element_type=jnp.float32
        )
        scores = (
            scores
            + lax.dot_general(flat_rope, block_rope, contract, preferred_element_type=jnp.float32)
        ) * score_scale
        allowed = (key_index[None, :] <= row_token[:, None]) & (
            key_request[None, :] == row_request[:, None]
        )
        scores = jnp.where(allowed, scores, MASKED)
        new_peak = jnp.maximum(peak_now, jnp.max(scores, axis=1))
        exp_terms = jnp.where(allowed, jnp.exp(scores - new_peak[:, None]), 0.0)
        fade_factor = jnp.exp(peak_now - new_peak)
        total_now = total_now * fade_factor + jnp.sum(exp_terms, axis=1)
        acc_now = acc_now * fade_factor[:, None] + jnp.dot(
            exp_terms.astype(jnp.bfloat16), block_latent, preferred_element_type=jnp.float32
        )
        return (new_peak, total_now, acc_now)

    run_peak, run_total, run_acc = lax.fori_loop(
        0, piece_rows // block_width, key_block, (run_peak, run_total, run_acc)
    )
    block_count = piece_rows // BLOCK
    pick_matrix = (
        source_block[:, None] == jnp.arange(block_count, dtype=jnp.int32)[None, :]
    ) & slot_filled[:, None]
    pick_matrix = pick_matrix.astype(jnp.bfloat16)
    slot_latent = jnp.dot(
        pick_matrix,
        piece_latent.reshape(block_count, BLOCK * KV_RANK),
        preferred_element_type=jnp.float32,
    )
    slot_rope = jnp.dot(
        pick_matrix,
        piece_rope.reshape(block_count, BLOCK * ROPE),
        preferred_element_type=jnp.float32,
    )
    folded = (run_peak, run_total, run_acc, slot_latent, slot_rope)
    run_total = folded[1]
    run_acc = folded[2]
    slot_latent = folded[3]
    slot_rope = folded[4]
    attended = (
        (run_acc / run_total[:, None]).astype(jnp.bfloat16).reshape(tok_rows, heads_here, KV_RANK)
    )
    head_out = jnp.einsum(
        "thc,hcv->thv", attended, value_up, preferred_element_type=jnp.float32
    ).astype(jnp.bfloat16)
    attn_part = jnp.dot(
        head_out.reshape(tok_rows, heads_here * V_HEAD),
        out_proj,
        preferred_element_type=jnp.float32,
    )
    mixed_rows = hidden.astype(jnp.float32) + lax.psum(
        attn_part.astype(jnp.bfloat16), "head"
    ).astype(jnp.float32)
    moe_in = rms_rows(mixed_rows, ffn_gain).astype(jnp.bfloat16)
    expert_count = router.shape[1]
    capacity = max(2, tok_rows * TOP * 4 // (3 * expert_count))
    gate_score = jax.nn.sigmoid(
        jnp.dot(moe_in.astype(jnp.float32), router, precision=lax.Precision.HIGHEST)
    )
    expert_axis = jnp.arange(expert_count, dtype=jnp.int32)
    id_match = expert_ids[:, :, None] == expert_axis[None, None, :]
    chosen = jnp.sum(jnp.where(id_match, gate_score[:, None, :], 0.0), axis=2)
    gate_weight = ROUTE_SCALE * chosen / jnp.sum(chosen, axis=1, keepdims=True)
    flat_ids = expert_ids.reshape(-1)
    one_hot = (flat_ids[:, None] == expert_axis[None, :]).astype(jnp.int32)
    earlier = jnp.cumsum(one_hot, axis=0) - one_hot
    slot_rank = jnp.sum(earlier * one_hot, axis=1)
    flat_slot = flat_ids * capacity + slot_rank
    owner_token = jnp.repeat(jnp.arange(tok_rows, dtype=jnp.int32), TOP)
    slot_token = jnp.zeros((expert_count * capacity,), jnp.int32).at[flat_slot].set(owner_token)
    slot_used = jnp.zeros((expert_count * capacity,), jnp.bool_).at[flat_slot].set(True)
    send_rows = jnp.where(
        slot_used[:, None], moe_in[slot_token], jnp.zeros((), jnp.bfloat16)
    ).reshape(expert_count, capacity, D)
    gate_up_local = expert_gate_up[0]
    down_local = expert_down[0]
    quarter_cols = D // head_count
    arrived = lax.all_to_all(send_rows, "seq", split_axis=0, concat_axis=0, tiled=True)
    sources, item_count, width_cols = arrived.shape
    flat_rows = arrived.reshape(sources * item_count, width_cols)
    gate_part = jnp.dot(flat_rows, gate_up_local[0], preferred_element_type=jnp.float32)
    up_part = jnp.dot(flat_rows, gate_up_local[1], preferred_element_type=jnp.float32)
    activated = (jax.nn.silu(gate_part) * up_part).astype(jnp.bfloat16)
    part_out = (
        jnp.dot(activated, down_local, preferred_element_type=jnp.float32)
        .astype(jnp.bfloat16)
        .reshape(sources, item_count, width_cols)
    )
    returned = lax.all_to_all(part_out, "seq", split_axis=0, concat_axis=0, tiled=True)
    back_cols = returned.shape[2]
    picked = returned.reshape(expert_count * capacity, back_cols)[flat_slot].reshape(
        tok_rows, TOP, back_cols
    )
    weighted = jnp.sum(picked.astype(jnp.float32) * gate_weight[:, :, None], axis=1)
    moe_out = lax.psum_scatter(
        weighted.astype(jnp.bfloat16), "head", scatter_dimension=1, tiled=True
    ).astype(jnp.float32)
    residual_part = lax.dynamic_slice_in_dim(mixed_rows, head_place * quarter_cols, quarter_cols, 1)
    output = (residual_part + moe_out).astype(jnp.bfloat16)
    decode_latent = slot_latent.astype(jnp.bfloat16).reshape(DEC_SLOTS, BLOCK, KV_RANK)
    decode_rope = slot_rope.astype(jnp.bfloat16)
    return (output, decode_latent, decode_rope)


def solution(mesh):
    placed = (
        P("seq", None),
        P("seq", "head"),
        P(),
        P(),
        P("seq", None),
        P(),
        P(),
        P(),
        P(),
        P("head", None, None),
        P("head", None, None),
        P("head", None),
        P(),
        P(),
        P("seq", None, None, "head"),
        P("seq", "head", None),
    )
    return jax.shard_map(
        body,
        mesh=mesh,
        in_specs=placed,
        out_specs=(P("seq", "head"), P(("seq", "head"), None, None), P(("seq", "head"), None)),
        check_vma=False,
    )
```

profile of v0, /device:TPU:0, one launch (start us, length us, event | category | flops | bytes accessed | tf_op | source)
XLA Modules:
  0.0 396.9 jit_solution(13828456274183690813)
XLA Ops:
  8.6 2.7 fusion.47
  19.5 47.0 %all_gather.7 = bf16[2048,64]{0,1:T(8,128)(2,1)} all-gather(bf16[128,64]{0,1:T(8,128)(2,1)S(1)} %pad_maximum_fusion.1), channel_id=1, replica_groups=mesh['seq'=16,'head'=2] {'seq'}, dimensions={0}, use_global_device_ids=true | all-gather | bytes 278528 | tf_op jit(solution)/shard_map/all_gather | solution.py:124
  78.1 3.4 all-gather.2.cloned.1.call-done
  81.4 4.0 %copy.49 = bf16[2048,512]{1,0:T(8,128)(2,1)} copy(bf16[2048,512]{0,1:T(8,128)(2,1)} %all-gather.2.cloned.1.call-done) | data formatting | bytes 4194304
  85.4 20.3 %while.20 = (s32[]{:T(128)}, f32[1024]{0:T(1024)S(1)}, f32[1024]{0:T(1024)S(1)}, f32[1024,512]{1,0:T(8,128)}, s32[1,2]{1,0:T(1,128)}, /*index=5*/bf16[2048,512]{...) while((s32[]{:T(128)}, f32[1024]{0:T(1024)S(1)}, ...), condition=%wide.region_11.12_spmd.clone, body=%wide.region_7.11_spmd.clone.sunk | while | flops 2303208448 | bytes 58217812 | solution.py:156
  105.7 2.0 fusion.44
  107.8 2.2 convolution_convert_fusion.4
  112.0 3.6 scatter_custom_fusion
  115.8 3.4 scatter_custom_fusion.1
  119.2 8.2 %all-reduce.2.cloned.1.call-done = bf16[128,2048]{1,0:T(8,128)(2,1)} async-done(((bf16[128,2048]{1,0:T(8,128)(2,1)}), bf16[128,2048]{1,0:T(8,128)(2,1)}) %all-reduce.2.cloned.1.call-update) | async-done | bytes 524304 | tf_op jit(solution)/shard_map/psum | solution.py:190
  127.4 2.3 convert_add_fusion
  131.2 6.0 %gather_fusion = bf16[1024,2048]{1,0:T(8,128)(2,1)} fusion(bf16[128,2048]{1,0:T(8,128)(2,1)S(1)} %multiply_convert_fusion.1, s32[1024]{0:T(1024)S(1)} %fusion.60), kind=kCustom, calls=%fused_computation | custom fusion | bytes 8392704 | tf_op jit(solution)/shard_map/gather | solution.py:212
  137.2 2.5 broadcast_select_fusion
  139.7 100.7 %all_to_all.10 = bf16[16,64,2048]{2,1,0:T(8,128)(2,1)S(1)} all-to-all(bf16[16,64,2048]{2,1,0:T(8,128)(2,1)S(1)} %broadcast_select_fusion), channel_id=1, replica_groups=mesh['seq'=16,'head'=2] {'seq'}, dimensions={0} | all-to-all | bytes 8388608 | tf_op jit(solution)/shard_map/all_to_all | solution.py:217
  242.4 6.6 %fusion.28 = f32[1024,704]{0,1:T(8,128)} fusion(bf16[1024,2048]{1,0:T(8,128)(2,1)S(1)} %bitcast.84, bf16[1,2,2048,704]{2,3,1,0:T(8,128)(2,1)} %param.32), kind=kOutput, calls=%fused_computation.40 | convolution fusion | flops 2952790016 | bytes 9961472 | tf_op jit(solution)/shard_map/dot_general | solution.py:221
  249.1 11.3 %convolution_convert_fusion.1 = bf16[1024,2048]{1,0:T(8,128)(2,1)} fusion(bf16[1,704,2048]{2,1,0:T(8,128)(2,1)S(1)} %copy-done, f32[1024,704]{0,1:T(8,128)} %fusion.28, bf16[1024,2048]{1,0:T(8,128)(2,1)} %bitcast.85, bf16[1,2,2048,704]{2,3,1,0:T(8,128)(2,1)} %param.32), kind=kOutput, calls=%fused_computation.38 | convolution fusion | flops 5912002560 | bytes 17039360 | tf_op jit(solution)/shard_map/dot_general | solution.py:224
  260.4 4.7 %all-to-all-start.1 = ((bf16[16,64,2048]{2,1,0:T(8,128)(2,1)}), bf16[16,64,2048]{2,1,0:T(8,128)(2,1)}, u32[]{:S(2)}, u32[]{:S(2)}) async-start(bf16[16,64,2048]{2,1,0:T(8,128)(2,1)} %bitcast.83), calls=%async_computation.1 | async-start | bytes 8388608 | tf_op jit(solution)/shard_map/all_to_all | solution.py:228
  266.0 77.5 %all-to-all-done.1 = bf16[16,64,2048]{2,1,0:T(8,128)(2,1)} async-done(((bf16[16,64,2048]{2,1,0:T(8,128)(2,1)}), bf16[16,64,2048]{2,1,0:T(8,128)(2,1)}, u32[]{:S(2)}, u32[]{:S(2)}) %all-to-all-start.1) | async-done | bytes 4194336 | tf_op jit(solution)/shard_map/all_to_all | solution.py:228
  343.5 9.8 %gather_fusion.1 = bf16[768,2048]{1,0:T(8,128)(2,1)} fusion(bf16[1024,2048]{1,0:T(8,128)(2,1)} %bitcast.18, s32[1024]{0:T(1024)S(1)} %pad_clamp_fusion), kind=kCustom, calls=%fused_computation.1 | custom fusion | bytes 6294528 | tf_op jit(solution)/shard_map/gather | solution.py:230
  353.4 6.6 %reshape.294 = f32[128,6,2048]{2,1,0:T(8,128)} reshape(bf16[768,2048]{1,0:T(8,128)(2,1)} %gather_fusion.1) | data formatting | bytes 9437184 | tf_op jit(solution)/shard_map/convert_element_type | solution.py:233
  359.9 7.5 %multiply_reduce_fusion = bf16[128,2048]{1,0:T(8,128)(2,1)} fusion(f32[128,6,2048]{2,1,0:T(8,128)} %reshape.294, f32[128,6]{1,0:T(8,128)S(1)} %copy.57), kind=kLoop, calls=%fused_computation.36 | loop fusion | flops 2883584 | bytes 6818816 | tf_op jit(solution)/shard_map/reduce_sum | solution.py:233
  370.6 4.2 %reshape.291 = bf16[128,8192]{1,0:T(8,128)(2,1)} reshape(bf16[2048,512]{1,0:T(8,128)(2,1)} %get-tuple-element.499) | data formatting | bytes 4194304 | tf_op jit(solution)/shard_map/reshape | solution.py:166
  374.8 2.0 convolution_convert_fusion
  377.5 11.0 %reduce-scatter.2.cloned.1.call-done = bf16[128,1024]{1,0:T(8,128)(2,1)} async-done(((bf16[128,2048]{1,0:T(8,128)(2,1)}), bf16[128,1024]{1,0:T(8,128)(2,1)}) %reduce-scatter.2.cloned.1.call-update) | async-done | bytes 262160 | tf_op jit(solution)/shard_map/reduce_scatter | solution.py:234
  (136 shorter events, 53.4 us)
Async XLA Ops:
  7.2 241.9 %copy-start = (bf16[1,704,2048]{2,1,0:T(8,128)(2,1)S(1)}, bf16[1,704,2048]{2,1,0:T(8,128)(2,1)}, u32[]{:S(2)}) copy-start(bf16[1,704,2048]{2,1,0:T(8,128)(2,1)} %param.33) | copy-start | bytes 8650756
  7.2 5.9 %copy-start.12 = (s32[128,6]{0,1:T(8,128)S(1)}, s32[128,6]{0,1:T(8,128)}, u32[]{:S(2)}) copy-start(s32[128,6]{0,1:T(8,128)} %param.22) | copy-start | bytes 9220
  7.2 6.8 %copy-start.17 = (s32[2]{0:T(128)S(1)}, s32[2]{0:T(128)}, u32[]{:S(2)}) copy-start(s32[2]{0:T(128)} %param.20) | copy-start | bytes 28
  7.2 11.4 %copy-start.16 = (s32[2]{0:T(128)S(1)}, s32[2]{0:T(128)}, u32[]{:S(2)}) copy-start(s32[2]{0:T(128)} %param.21) | copy-start | bytes 28
  7.2 74.2 %all-gather.2.cloned.1.call-start = ((), (), s32[]{:S(2)}) async-start(), calls=%async_computation.3 | async-start | bytes 2228224 | tf_op jit(solution)/shard_map/all_gather | solution.py:123
  13.0 114.4 %all-reduce.2.cloned.1.call-start = ((), (), s32[]{:S(2)}) async-start(), calls=%async_computation.4 | async-start | bytes 1048576 | tf_op jit(solution)/shard_map/psum | solution.py:190
  73.8 3.4 copy-start.8
  73.8 3.4 copy-start.9
  87.0 1.8 copy-start.3
  87.0 1.9 copy-start.10
  90.7 1.6 copy-start.6
  97.2 1.8 copy-start.3
  97.2 1.9 copy-start.10
  105.7 5.8 %copy-start.1 = (bf16[2048,64]{1,0:T(8,128)(2,1)}, bf16[2048,64]{1,0:T(8,128)(2,1)S(1)}, u32[]{:S(2)}) copy-start(bf16[2048,64]{1,0:T(8,128)(2,1)S(1)} %get-tuple-element.498) | copy-start | bytes 786436
  105.7 4.3 %copy-start.4 = (bf16[1024,2048]{1,0:T(8,128)(2,1)S(1)}, bf16[1024,2048]{1,0:T(8,128)(2,1)}, u32[]{:S(2)}) copy-start(bf16[1024,2048]{1,0:T(8,128)(2,1)} %param.29) | copy-start | bytes 12582916
  107.8 4.1 %copy-start.13 = (s32[768]{0:T(1024)S(1)}, s32[768]{0:T(1024)}, u32[]{:S(2)}) copy-start(s32[768]{0:T(1024)} %eq.123) | copy-start | bytes 9220
  107.8 4.2 %copy-start.14 = (s32[768,1]{0,1:T(1,128)S(1)}, s32[768,1]{0,1:T(1,128)}, u32[]{:S(2)}) copy-start(s32[768,1]{0,1:T(1,128)} %mul.268) | copy-start | bytes 9220
  110.0 19.8 %copy-start.15 = (f32[2048]{0:T(1024)S(1)}, f32[2048]{0:T(1024)}, u32[]{:S(2)}) copy-start(f32[2048]{0:T(1024)} %param.30) | copy-start | bytes 24580
  240.5 2.0 copy-start.5
  260.4 5.0 %copy-start.11 = (f32[2048,16]{0,1:T(8,128)S(1)}, f32[2048,16]{0,1:T(8,128)}, u32[]{:S(2)}) copy-start(f32[2048,16]{0,1:T(8,128)} %param.31) | copy-start | bytes 393220
  260.4 83.2 %all-to-all-start.1 = ((bf16[16,64,2048]{2,1,0:T(8,128)(2,1)}), bf16[16,64,2048]{2,1,0:T(8,128)(2,1)}, u32[]{:S(2)}, u32[]{:S(2)}) async-start(bf16[16,64,2048]{2,1,0:T(8,128)(2,1)} %bitcast.83), calls=%async_computation.1 | async-start | bytes 8388608 | tf_op jit(solution)/shard_map/all_to_all | solution.py:228
  265.0 123.5 %reduce-scatter.2.cloned.1.call-start = ((), (), s32[]{:S(2)}) async-start(), calls=%async_computation.5 | async-start | bytes 786432 | tf_op jit(solution)/shard_map/reduce_scatter | solution.py:234
  359.9 7.5 %copy-start.2 = (bf16[2048,64]{1,0:T(8,128)(2,1)S(1)}, bf16[2048,64]{1,0:T(8,128)(2,1)}, u32[]{:S(2)}) copy-start(bf16[2048,64]{1,0:T(8,128)(2,1)} %copy-done.1) | copy-start | bytes 786436
  359.9 8.6 %copy-start.18 = (s32[128]{0:T(128)S(1)}, s32[128]{0:T(128)}, u32[]{:S(2)}) copy-start(s32[128]{0:T(128)} %param.23) | copy-start | bytes 1540
  (3 other events, 4.3 us)
Sparse Core Ops, SparseCore 0:
  13.1 68.2 all-gather.1
  111.7 15.6 all-reduce.1
  367.5 20.9 reduce-scatter.1
where the time goes:
time: 399 us; the launch traced here: 397 us
  blocking collectives  148 us (37%)
  waiting for transfers between devices  100 us (25%)
  local copies, waits for them, and re-layouts  56 us (14%)
  matrix products  41.4 us (10%)
  other arithmetic  32.5 us (8%)
  between operations  14 us (4%)
  starting transfers between devices  5 us (1%)
    all_to_all x1, blocking collectives, body(): lax.all_to_all(send_rows, 'seq', split_axis=0, concat_axis=0, tiled=True)  101 us
    all_to_all x1, waiting for transfers between devices, body(): lax.all_to_all(part_out, 'seq', split_axis=0, concat_axis=0, tiled=True)  77.5 us
    all_gather x1, blocking collectives, body(): piece_rope = lax.all_gather(key_rope, 'seq', axis=0, tiled=True)  47 us
    dot_general x1, matrix products, body(): jnp.dot(activated, down_local, preferred_element_type=jnp.float32)  11.3 us
    reduce_scatter x1, waiting for transfers between devices, body(): lax.psum_scatter(weighted.astype(jnp.bfloat16), 'head', scatter_dimension...  11 us
    unnamed x35, local copies, waits for them, and re-layouts  9.92 us
    gather x1, local copies, waits for them, and re-layouts, body(): returned.reshape(expert_count * capacity, back_cols)[flat_slot]  9.82 us
    psum x1, waiting for transfers between devices, body(): lax.psum(attn_part.astype(jnp.bfloat16), 'head').astype(jnp.float32)  8.21 us
  transfers between devices with their start and end apart: 4, of which 4 were waited for; matrix products, arithmetic and copies ran while one was open for 9% of the time, Pallas kernels for 0%

commit v1 on v0

--- a/solution.py
+++ b/solution.py
@@ -1,8 +1,11 @@
+import functools
 import math
 
 import jax
 import jax.numpy as jnp
 from jax import lax
+from jax.experimental import pallas as pl
+from jax.experimental.pallas import tpu as pltpu
 from jax.sharding import PartitionSpec as P
 
 D = 2048
@@ -49,14 +52,26 @@
     )
 
 
+def running(lengths):
+    index = jnp.arange(lengths.shape[0])
+    return jnp.sum(jnp.where(index[None, :] <= index[:, None], lengths[None, :], 0), axis=1)
+
+
+def ranks(member):
+    count = member.shape[-1]
+    index = jnp.arange(count)
+    before = (index[:, None] < index[None, :]).astype(jnp.bfloat16)
+    return jnp.dot(member, before, preferred_element_type=jnp.float32).astype(jnp.int32)
+
+
 def request_of(req_len, token_index):
-    req_ends = jnp.cumsum(req_len)
+    req_ends = running(req_len)
     return jnp.sum((token_index[:, None] >= req_ends[None, :]).astype(jnp.int32), axis=1)
 
 
 def position_of(req_len, req_offset, token_index):
     request = request_of(req_len, token_index)
-    req_ends = jnp.cumsum(req_len)
+    req_ends = running(req_len)
     starts = req_ends - req_len
     member = request[:, None] == jnp.arange(req_len.shape[0])[None, :]
     start_at = jnp.sum(jnp.where(member, starts[None, :], 0), axis=1)
@@ -68,6 +83,406 @@
     for option_width in (1024, 512, 256, 128):
         return option_width
     return piece_rows
+
+
+MESH = pl.DeviceIdType.MESH
+
+
+def flip(place, step):
+    return place + step * (1 - 2 * lax.rem(lax.div(place, step), 2))
+
+
+def place_of(s, h, nz, back, turn):
+    line = lax.rem(lax.div(s, 4) - back + nz, nz)
+    block = line * 4 + lax.rem(s, 4)
+    if turn & 1:
+        block = flip(block, 2 - h)
+    if turn & 2:
+        block = flip(block, 1 + h)
+    return block
+
+
+def meet(s, h, nz):
+    barrier = pltpu.get_barrier_semaphore()
+    peers = [(place_of(s, h, nz, back, 0), h) for back in range(1, nz)]
+    peers += [(flip(s, 2 - h), h), (flip(s, 1 + h), h), (s, 1 - h)]
+    for peer in peers:
+        pl.semaphore_signal(barrier, inc=1, device_id=peer, device_id_type=MESH)
+    pl.semaphore_wait(barrier, len(peers))
+
+
+class Spread:
+    def __init__(self, buf, s, h, nz, sems):
+        self.buf, self.s, self.h, self.nz = buf, s, h, nz
+        self.sems = sems
+
+    def move(self, block, kind, index, device):
+        view = self.buf.at[self.h, block]
+        return pltpu.make_async_remote_copy(
+            src_ref=view,
+            dst_ref=view,
+            send_sem=self.sems[2 * kind].at[index],
+            recv_sem=self.sems[2 * kind + 1].at[index],
+            device_id=device,
+            device_id_type=MESH,
+        )
+
+    def block(self, back, turn):
+        return place_of(self.s, self.h, self.nz, back, turn)
+
+    def line(self, ahead):
+        device = (place_of(self.s, self.h, self.nz, self.nz - ahead, 0), self.h)
+        return self.move(self.block(0, 0), 0, ahead, device)
+
+    def line_in(self, back):
+        return self.move(self.block(back, 0), 0, back, (self.s, 1 - self.h))
+
+    def second(self, back, turn=0):
+        return self.move(self.block(back, turn), 1, back, (flip(self.s, 2 - self.h), self.h))
+
+    def third(self, back, side, turn=0):
+        device = (flip(self.s, 1 + self.h), self.h)
+        return self.move(self.block(back, turn + side), 2, 2 * back + side, device)
+
+    def sibling(self, back, mine):
+        half = self.h if mine else 1 - self.h
+        line = lax.rem(lax.div(self.s, 4) - back + self.nz, self.nz)
+        view = self.buf.at[half, pl.ds(line * 4, 4)]
+        return pltpu.make_async_remote_copy(
+            src_ref=view,
+            dst_ref=view,
+            send_sem=self.sems[6].at[back],
+            recv_sem=self.sems[7].at[back],
+            device_id=(self.s, 1 - self.h),
+            device_id_type=MESH,
+        )
+
+    def send_all(self):
+        for ahead in range(1, self.nz):
+            self.line(ahead).start()
+        for back in range(self.nz):
+            if back:
+                self.line_in(back).wait_recv()
+            self.third(back, 0).start()
+            self.second(back).start()
+            self.second(back, 1).wait_recv()
+            self.third(back, 1).start()
+
+    def pass_on(self, back):
+        for side in range(2):
+            self.third(back, side, 2).wait_recv()
+        self.sibling(back, True).start()
+
+    def drain(self):
+        for ahead in range(1, self.nz):
+            self.line(ahead).wait_send()
+        for back in range(self.nz):
+            self.second(back).wait_send()
+            self.third(back, 0).wait_send()
+            self.third(back, 1).wait_send()
+            self.sibling(back, True).wait_send()
+
+
+def spread_sems(nz):
+    dma = pltpu.SemaphoreType.DMA
+    return [dma((nz,)), dma((nz,)), dma((nz,)), dma((nz,)), dma((2 * nz,)), dma((2 * nz,)), dma((nz,)), dma((nz,))]
+
+
+def gather_kernel(nz, rows_ref, out_ref, *sems):
+    s, h = lax.axis_index("seq"), lax.axis_index("head")
+    half = rows_ref.shape[1]
+    out_ref[h, s] = rows_ref[h]
+    meet(s, h, nz)
+    spread = Spread(out_ref, s, h, nz, sems)
+    spread.send_all()
+    for back in range(nz):
+        spread.pass_on(back)
+    for back in range(nz):
+        spread.sibling(back, False).wait_recv()
+    spread.drain()
+
+
+def gather_rows(rows, seq_count):
+    tok_rows, width = rows.shape
+    nz = seq_count // 4
+    out = pl.pallas_call(
+        functools.partial(gather_kernel, nz),
+        out_shape=jax.ShapeDtypeStruct((2, seq_count, tok_rows // 2, width), rows.dtype),
+        in_specs=[pl.BlockSpec(memory_space=pltpu.VMEM)],
+        out_specs=pl.BlockSpec(memory_space=pltpu.VMEM),
+        scratch_shapes=spread_sems(nz),
+        compiler_params=pltpu.CompilerParams(
+            collective_id=0, has_side_effects=True, vmem_limit_bytes=16 * 1024 * 1024
+        ),
+    )(rows.reshape(2, tok_rows // 2, width))
+    return jnp.swapaxes(out, 0, 1).reshape(seq_count * tok_rows, width)
+
+
+def expert_kernel(
+    nz,
+    hidden_ref,
+    attn_ref,
+    gain_ref,
+    pick_ref,
+    place_ref,
+    chosen_ref,
+    router_ref,
+    gate_up_hbm,
+    down_hbm,
+    out_ref,
+    attn_in,
+    mixed,
+    x_buf,
+    part,
+    sib_buf,
+    t3_buf,
+    t2_buf,
+    t1_buf,
+    gate_up,
+    down,
+    rows_buf,
+    act_buf,
+    res_buf,
+    load_sem,
+    attn_sem,
+    e0_send,
+    e0_recv,
+    e3_send,
+    e3_recv,
+    e2_send,
+    e2_recv,
+    e1_send,
+    e1_recv,
+    *sems,
+):
+    s, h = lax.axis_index("seq"), lax.axis_index("head")
+    cols = hidden_ref.shape[1]
+    half = cols // 2
+    slots = pick_ref.shape[1]
+    loads = [
+        pltpu.make_async_copy(gate_up_hbm, gate_up, load_sem.at[0]),
+        pltpu.make_async_copy(down_hbm, down, load_sem.at[1]),
+    ]
+    for load in loads:
+        load.start()
+    meet(s, h, nz)
+    swap = pltpu.make_async_remote_copy(
+        src_ref=attn_ref,
+        dst_ref=attn_in,
+        send_sem=attn_sem.at[0],
+        recv_sem=attn_sem.at[1],
+        device_id=(s, 1 - h),
+        device_id_type=MESH,
+    )
+    swap.start()
+    swap.wait_recv()
+    total = hidden_ref[...].astype(jnp.float32) + (
+        attn_ref[...].astype(jnp.float32) + attn_in[...].astype(jnp.float32)
+    )
+    mixed[0] = total[:, :half]
+    mixed[1] = total[:, half:]
+    inverse = lax.rsqrt(jnp.mean(total * total, axis=1, keepdims=True) + EPSILON)
+    x_buf[h, s] = (mixed[h] * inverse * gain_ref[h][None, :]).astype(jnp.bfloat16)
+    spread = Spread(x_buf, s, h, nz, sems)
+    spread.send_all()
+    spread.pass_on(0)
+    for load in loads:
+        load.wait()
+
+    def remote(src, dst, send, recv, index, device):
+        return pltpu.make_async_remote_copy(
+            src_ref=src,
+            dst_ref=dst,
+            send_sem=send.at[index],
+            recv_sem=recv.at[index],
+            device_id=device,
+            device_id_type=MESH,
+        )
+
+    sibling = (s, 1 - h)
+    partner2 = (flip(s, 2 - h), h)
+    partner3 = (flip(s, 1 + h), h)
+
+    def line_of(back):
+        return lax.rem(lax.div(s, 4) - back + nz, nz)
+
+    def give0(back):
+        base = pl.ds(line_of(back) * 4, 4)
+        return remote(part.at[1 - h, base], sib_buf.at[base], e0_send, e0_recv, back, sibling)
+
+    def give3(back, side):
+        block = place_of(s, h, nz, back, 2 + side)
+        index = 2 * back + side
+        return remote(part.at[h, block], t3_buf.at[index], e3_send, e3_recv, index, partner3)
+
+    def give2(back):
+        block = place_of(s, h, nz, back, 1)
+        return remote(part.at[h, block], t2_buf.at[back], e2_send, e2_recv, back, partner2)
+
+    def give1(back):
+        block = place_of(s, h, nz, back, 0)
+        return remote(part.at[h, block], t1_buf.at[back], e1_send, e1_recv, back, (block, h))
+
+    def add(block, other):
+        part[h, block] = (
+            part[h, block].astype(jnp.float32) + other.astype(jnp.float32)
+        ).astype(jnp.bfloat16)
+
+    def feed(back):
+        spread.sibling(back, False).wait_recv()
+        base = line_of(back) * 4
+        for c in range(4):
+            pick = pick_ref[base + c]
+            for side in range(2):
+                rows_buf[c * slots : (c + 1) * slots, side * half : (side + 1) * half] = jnp.dot(
+                    pick, x_buf[side, base + c], preferred_element_type=jnp.float32
+                ).astype(jnp.bfloat16)
+        rows = rows_buf[...]
+        logit = jnp.dot(rows, router_ref[...], preferred_element_type=jnp.float32)
+        width = logit.shape[1] // 3
+        logit = logit[:, :width] + (logit[:, width : 2 * width] + logit[:, 2 * width :])
+        score = 1.0 / (1.0 + jnp.exp(-logit))
+        chosen = score * chosen_ref[pl.ds(base, 4)].reshape(4 * slots, width)
+        own = jnp.where(lax.broadcasted_iota(jnp.int32, chosen.shape, 1) == s, chosen, 0.0)
+        own = jnp.sum(own, axis=1, keepdims=True)
+        every = jnp.sum(chosen, axis=1, keepdims=True)
+        weight = ROUTE_SCALE * own / jnp.where(every > 0.0, every, 1.0)
+        gate = jnp.dot(rows, gate_up[0], preferred_element_type=jnp.float32)
+        up = jnp.dot(rows, gate_up[1], preferred_element_type=jnp.float32)
+        act_buf[...] = (gate / (1.0 + jnp.exp(-gate)) * up * weight).astype(jnp.bfloat16)
+        res_buf[...] = jnp.dot(
+            act_buf[...], down[...], preferred_element_type=jnp.float32
+        ).astype(jnp.bfloat16)
+        for c in range(4):
+            for side in range(2):
+                part[side, base + c] = jnp.dot(
+                    place_ref[base + c],
+                    res_buf[c * slots : (c + 1) * slots, side * half : (side + 1) * half],
+                    preferred_element_type=jnp.float32,
+                ).astype(jnp.bfloat16)
+        give0(back).start()
+
+    def fold0(back):
+        give0(back).wait_recv()
+        for turn in (2, 3, 1, 0):
+            block = place_of(s, h, nz, back, turn)
+            add(block, sib_buf[block])
+            if turn >= 2:
+                give3(back, turn - 2).start()
+
+    def fold3(back):
+        for side in (1, 0):
+            give3(back, side).wait_recv()
+            add(place_of(s, h, nz, back, side), t3_buf[2 * back + side])
+            if side:
+                give2(back).start()
+
+    def fold2(back):
+        give2(back).wait_recv()
+        add(place_of(s, h, nz, back, 0), t2_buf[back])
+
+        @pl.when(back > 0)
+        def _():
+            give1(back).start()
+
+    @pl.loop(0, nz + 3)
+    def _(step):
+        @pl.when(step < nz)
+        def _():
+            feed(step)
+
+        @pl.when(step < nz - 1)
+        def _():
+            spread.pass_on(step + 1)
+
+        @pl.when((step >= 3))
+        def _():
+            fold2(step - 3)
+
+        @pl.when((step >= 2) & (step < nz + 2))
+        def _():
+            fold3(step - 2)
+
+        @pl.when((step >= 1) & (step < nz + 1))
+        def _():
+            fold0(step - 1)
+
+    result = mixed[h] + part[h, s].astype(jnp.float32)
+    for back in range(1, nz):
+        give1(back).wait_recv()
+        result = result + t1_buf[back].astype(jnp.float32)
+    out_ref[...] = result.astype(out_ref.dtype)
+    swap.wait_send()
+    spread.drain()
+    for back in range(nz):
+        give0(back).wait_send()
+        give3(back, 0).wait_send()
+        give3(back, 1).wait_send()
+        give2(back).wait_send()
+        if back:
+            give1(back).wait_send()
+
+
+def expert_layer(hidden, attn_part, masks, ffn_gain, router, gate_up, down, seq_place, seq_count):
+    tok_rows, cols = hidden.shape
+    half = cols // 2
+    nz = seq_count // 4
+    expert_count = router.shape[1]
+    hidden_units = down.shape[0]
+    capacity = max(2, tok_rows * TOP * 4 // (3 * expert_count))
+    mine = lax.dynamic_index_in_dim(masks, seq_place, 2, keepdims=False)
+    rank = ranks(mine)
+    slot = jnp.arange(capacity, dtype=jnp.int32)
+    pick = (rank[:, None, :] == slot[None, :, None]) & (mine[:, None, :] > 0)
+    pick = pick.astype(jnp.bfloat16)
+    place = (rank[:, :, None] == slot[None, None, :]) & (mine[:, :, None] > 0)
+    place = place.astype(jnp.bfloat16)
+    wide_masks = jnp.pad(masks, ((0, 0), (0, 0), (0, 128 - expert_count)))
+    chosen = jnp.einsum("brt,bte->bre", pick, wide_masks, preferred_element_type=jnp.float32)
+    router = jnp.pad(router, ((0, 0), (0, 128 - expert_count)))
+    high = lax.reduce_precision(router, 8, 7)
+    middle = lax.reduce_precision(router - high, 8, 7)
+    low = router - high - middle
+    router3 = jnp.concatenate([high, middle, low], axis=1).astype(jnp.bfloat16)
+    vmem = pl.BlockSpec(memory_space=pltpu.VMEM)
+    hbm = pl.BlockSpec(memory_space=pl.ANY)
+    dma = pltpu.SemaphoreType.DMA
+    bf16 = jnp.bfloat16
+    return pl.pallas_call(
+        functools.partial(expert_kernel, nz),
+        out_shape=jax.ShapeDtypeStruct((tok_rows, half), bf16),
+        in_specs=[vmem] * 7 + [hbm] * 2,
+        out_specs=vmem,
+        scratch_shapes=[
+            pltpu.VMEM((tok_rows, cols), bf16),
+            pltpu.VMEM((2, tok_rows, half), jnp.float32),
+            pltpu.VMEM((2, seq_count, tok_rows, half), bf16),
+            pltpu.VMEM((2, seq_count, tok_rows, half), bf16),
+            pltpu.VMEM((seq_count, tok_rows, half), bf16),
+            pltpu.VMEM((2 * nz, tok_rows, half), bf16),
+            pltpu.VMEM((nz, tok_rows, half), bf16),
+            pltpu.VMEM((nz, tok_rows, half), bf16),
+            pltpu.VMEM(gate_up.shape, bf16),
+            pltpu.VMEM(down.shape, bf16),
+            pltpu.VMEM((4 * capacity, cols), bf16),
+            pltpu.VMEM((4 * capacity, hidden_units), bf16),
+            pltpu.VMEM((4 * capacity, cols), bf16),
+            dma((2,)),
+            dma((2,)),
+            dma((nz,)),
+            dma((nz,)),
+            dma((2 * nz,)),
+            dma((2 * nz,)),
+            dma((nz,)),
+            dma((nz,)),
+            dma((nz,)),
+            dma((nz,)),
+        ]
+        + spread_sems(nz),
+        compiler_params=pltpu.CompilerParams(
+            collective_id=1, has_side_effects=True, vmem_limit_bytes=56 * 1024 * 1024
+        ),
+    )(hidden, attn_part, ffn_gain.reshape(2, half), pick, place, chosen, router3, gate_up, down)
 
 
 def body(
@@ -120,8 +535,21 @@
     run_peak = jnp.full((query_rows,), MASKED, jnp.float32)
     run_total = jnp.zeros((query_rows,), jnp.float32)
     run_acc = jnp.zeros((query_rows, KV_RANK), jnp.float32)
-    piece_latent = lax.all_gather(latent, "seq", axis=0, tiled=True)
-    piece_rope = lax.all_gather(key_rope, "seq", axis=0, tiled=True)
+    expert_count = router.shape[1]
+    expert_axis = jnp.arange(expert_count, dtype=jnp.int32)
+    seq_count = lax.axis_size("seq")
+    fast = seq_count % 4 == 0 and seq_count <= 16 and head_count == 2 and expert_count <= 64
+    if fast:
+        route_mask = jnp.any(expert_ids[:, :, None] == expert_axis[None, None, :], axis=1)
+        payload = jnp.concatenate([latent, key_rope, route_mask.astype(jnp.bfloat16)], axis=1)
+        payload = jnp.pad(payload, ((0, 0), (0, -payload.shape[1] % 128)))
+        gathered = gather_rows(payload, seq_count)
+        piece_latent = gathered[:, :KV_RANK]
+        piece_rope = gathered[:, KV_RANK : KV_RANK + ROPE]
+        all_masks = gathered[:, KV_RANK + ROPE : KV_RANK + ROPE + expert_count]
+    else:
+        piece_latent = lax.all_gather(latent, "seq", axis=0, tiled=True)
+        piece_rope = lax.all_gather(key_rope, "seq", axis=0, tiled=True)
     piece_rows = piece_latent.shape[0]
     block_width = key_width(piece_rows)
 
@@ -187,22 +615,35 @@
         out_proj,
         preferred_element_type=jnp.float32,
     )
+    decode_latent = slot_latent.astype(jnp.bfloat16).reshape(DEC_SLOTS, BLOCK, KV_RANK)
+    decode_rope = slot_rope.astype(jnp.bfloat16)
+    if fast:
+        output = expert_layer(
+            hidden,
+            attn_part.astype(jnp.bfloat16),
+            all_masks.reshape(seq_count, tok_rows, expert_count),
+            ffn_gain,
+            router,
+            expert_gate_up[0],
+            expert_down[0],
+            seq_place,
+            seq_count,
+        )
+        return (output, decode_latent, decode_rope)
     mixed_rows = hidden.astype(jnp.float32) + lax.psum(
         attn_part.astype(jnp.bfloat16), "head"
     ).astype(jnp.float32)
     moe_in = rms_rows(mixed_rows, ffn_gain).astype(jnp.bfloat16)
-    expert_count = router.shape[1]
     capacity = max(2, tok_rows * TOP * 4 // (3 * expert_count))
     gate_score = jax.nn.sigmoid(
         jnp.dot(moe_in.astype(jnp.float32), router, precision=lax.Precision.HIGHEST)
     )
-    expert_axis = jnp.arange(expert_count, dtype=jnp.int32)
     id_match = expert_ids[:, :, None] == expert_axis[None, None, :]
     chosen = jnp.sum(jnp.where(id_match, gate_score[:, None, :], 0.0), axis=2)
     gate_weight = ROUTE_SCALE * chosen / jnp.sum(chosen, axis=1, keepdims=True)
     flat_ids = expert_ids.reshape(-1)
     one_hot = (flat_ids[:, None] == expert_axis[None, :]).astype(jnp.int32)
-    earlier = jnp.cumsum(one_hot, axis=0) - one_hot
+    earlier = ranks(one_hot.T.astype(jnp.bfloat16)).T
     slot_rank = jnp.sum(earlier * one_hot, axis=1)
     flat_slot = flat_ids * capacity + slot_rank
     owner_token = jnp.repeat(jnp.arange(tok_rows, dtype=jnp.int32), TOP)
@@ -236,8 +677,6 @@
     ).astype(jnp.float32)
     residual_part = lax.dynamic_slice_in_dim(mixed_rows, head_place * quarter_cols, quarter_cols, 1)
     output = (residual_part + moe_out).astype(jnp.bfloat16)
-    decode_latent = slot_latent.astype(jnp.bfloat16).reshape(DEC_SLOTS, BLOCK, KV_RANK)
-    decode_rope = slot_rope.astype(jnp.bfloat16)
     return (output, decode_latent, decode_rope)
 
 

time: 399 us -> 231 us (0.58)
  blocking collectives: 148 us -> 0 us
  Pallas kernels: 0 us -> 142 us
  waiting for transfers between devices: 100 us -> 0 us
  local copies, waits for them, and re-layouts: 56 us -> 29.2 us
  between operations: 14 us -> 0.93 us
  other arithmetic: 32.5 us -> 20 us
  starting transfers between devices: 5 us -> 0 us
    pallas_call x0 -> x2, Pallas kernels: none -> 142 us  [the longest x1 115 us: expert_layer(): pl.pallas_call(functools.partial(expert_kernel, nz), out_shape=jax.ShapeD...]
    all_to_all x1 -> x0, blocking collectives: 101 us -> none  [body(): lax.all_to_all(send_rows, 'seq', split_axis=0, concat_axis=0, tiled=True)]
    all_to_all x1 -> x0, waiting for transfers between devices: 77.5 us -> none  [body(): lax.all_to_all(part_out, 'seq', split_axis=0, concat_axis=0, tiled=True)]
    all_gather x1 -> x0, blocking collectives: 47 us -> none  [body(): piece_rope = lax.all_gather(key_rope, 'seq', axis=0, tiled=True)]
    dot_general x3 -> x2, matrix products: 18.4 us -> 1.2 us  [the longest x1 1.07 us: expert_layer(): jnp.einsum('brt,bte->bre', pick, wide_masks, preferred_element_type=jnp.f...]
    gather x2 -> x0, local copies, waits for them, and re-layouts: 15.8 us -> none  [the longest x1 9.82 us: body(): returned.reshape(expert_count * capacity, back_cols)[flat_slot]]
    reduce_scatter x1 -> x0, waiting for transfers between devices: 11 us -> none  [body(): lax.psum_scatter(weighted.astype(jnp.bfloat16), 'head', scatter_dimension...]
    dot_general x2, matrix products: 3.49 us -> 12.8 us  [key_block(): lax.dot_general(flat_latent, block_latent, contract, preferred_element_ty...]
  transfers between devices with their start and end apart: 4 -> 0, of which waited for: 4 -> 0; matrix products, arithmetic and copies ran while one was open for 9% -> 0% of each run, Pallas kernels for 0% -> 0%
where the time goes in v1:
time: 231 us; the launch traced here: 230 us
  Pallas kernels  142 us (61%)
  matrix products  37.5 us (16%)
  local copies, waits for them, and re-layouts  29.2 us (13%)
  other arithmetic  20 us (9%)
    pallas_call x1, Pallas kernels, expert_layer(): pl.pallas_call(functools.partial(expert_kernel, nz), out_shape=jax.ShapeD...  115 us
    pallas_call x1, Pallas kernels, gather_rows(): pl.pallas_call(functools.partial(gather_kernel, nz), out_shape=jax.ShapeD...  26.8 us
    unnamed x32, local copies, waits for them, and re-layouts  14.2 us
    dot_general x2, matrix products, key_block(): lax.dot_general(flat_latent, block_latent, contract, preferred_element_ty...  12.8 us
    dot_general x2, matrix products, key_block(): jnp.dot(exp_terms.astype(jnp.bfloat16), block_latent, preferred_element_t...  9.18 us
    reduce_sum x2, other arithmetic, key_block(): total_now = total_now * fade_factor + jnp.sum(exp_terms, axis=1)  6.19 us
    dot_general x2, matrix products, key_block(): lax.dot_general(flat_rope, block_rope, contract, preferred_element_type=j...  5.27 us

profile of v1, /device:TPU:0, one launch (start us, length us, event | category | flops | bytes accessed | tf_op | source)
XLA Modules:
  0.0 229.8 jit_solution(10369247656533448014)
XLA Ops:
  4.4 1.9 fusion.37
  6.9 26.8 %shard_map.175 = bf16[2,16,64,640]{3,2,1,0:T(8,128)(2,1)S(1)} custom-call(bf16[2,64,640]{2,1,0:T(8,128)(2,1)S(1)} %bitcast.40), custom_call_target="tpu_custom_call" | custom-call | tf_op jit(solution)/shard_map/pallas_call | solution.py:208
  34.1 1.5 copy-done.2
  41.7 3.1 %slice.45 = bf16[2048,512]{1,0:T(8,128)(2,1)} slice(bf16[2048,640]{1,0:T(8,128)(2,1)} %bitcast.43), slice={[0:2048], [0:512]} | slice | bytes 4194304 | tf_op jit(solution)/shard_map/slice | solution.py:547
  46.4 1.6 copy.58
  48.0 35.4 %while.18 = (s32[]{:T(128)}, f32[1024]{0:T(1024)S(1)}, f32[1024]{0:T(1024)S(1)}, f32[1024,512]{1,0:T(8,128)}, s32[2]{0:T(128)}, /*index=5*/bf16[2048,512]{1,0:T(...) while((s32[]{:T(128)}, f32[1024]{0:T(1024)S(1)}, ...), condition=%wide.region_12.13_spmd.clone, body=%wide.region_7.12_spmd.clone.sunk | while | flops 2303208448 | bytes 45768032 | solution.py:584
  48.0 2.6 %fusion.93 = f32[1024,1024]{1,0:T(8,128)} fusion(bf16[1024,64]{1,0:T(8,128)(2,1)S(1)} %get-tuple-element.384, bf16[2048,64]{1,0:T(8,128)(2,1)S(1)} %get-tuple-element.383, s32[]{:T(128)S(6)} %select_n.87), kind=kOutput, calls=%fused_computation.18.clone.1 | convolution fusion | flops 134217728 | bytes 4718596 | tf_op jit(solution)/shard_map/while/body/eval_jaxpr/dot_general | solution.py:569
  51.3 6.4 %fusion.96 = (f32[1024]{0:T(1024)S(1)}, f32[1024,1024]{0,1:T(8,128)}) fusion(f32[1024,1024]{1,0:T(8,128)} %fusion.93, bf16[1024,512]{1,0:T(8,128)(2,1)} %get-tuple-element.382, bf16[2048,512]{1,0:T(8,128)(2,1)} %get-tuple-element.381, s32[]{:T(128)S(6)} %select_n.87, s32[1024]{0:T(1024)S(1)} %eq.243, s32[1024]{0:T(1024)S(1)} %fusion.95, ...), kind=kOutput, calls=%fused_computation.115.clone.1 | convolution fusion | flops 1081080832 | bytes 10506244 | tf_op jit(solution)/shard_map/while/body/eval_jaxpr/dot_general | solution.py:564
  57.7 3.1 %fusion.97 = f32[1024]{0:T(1024)S(1)} fusion(f32[1024,1024]{0,1:T(8,128)} %get-tuple-element.343, f32[1024]{0:T(1024)S(1)} %select_maximum_fusion.2, s32[1024]{0:T(1024)S(1)} %eq.243, s32[1024]{0:T(1024)S(1)} %le.162, s32[1024]{0:T(1024)S(1)} %fusion.95, s32[1024]{0:T(1024)S(1)} %iota_add_fusion.4), kind=kLoop, calls=%fused_computation.6.clone.1 | loop fusion | flops 6290432 | bytes 4218880 | tf_op jit(solution)/shard_map/while/body/eval_jaxpr/reduce_sum | solution.py:578
  61.1 4.2 %fusion.99 = f32[1024,512]{1,0:T(8,128)} fusion(f32[1024,512]{1,0:T(8,128)} %get-tuple-element.364, f32[1024,1024]{0,1:T(8,128)S(1)} %copy-done.1, f32[1024]{0:T(1024)S(1)} %select_maximum_fusion.2, s32[1024]{0:T(1024)S(1)} %eq.243, s32[1024]{0:T(1024)S(1)} %le.162, s32[1024]{0:T(1024)S(1)} %fusion.95, s32[1024]{0:T(1024)S(1)} %iota_add_fusion.4, ...), kind=kOutput, calls=%fused_computation.9.clone.1 | convolution fusion | flops 1081606144 | bytes 9461765 | tf_op jit(solution)/shard_map/while/body/eval_jaxpr/dot_general | solution.py:579
  65.4 2.6 %fusion.93 = f32[1024,1024]{1,0:T(8,128)} fusion(bf16[1024,64]{1,0:T(8,128)(2,1)S(1)} %get-tuple-element.384, bf16[2048,64]{1,0:T(8,128)(2,1)S(1)} %get-tuple-element.383, s32[]{:T(128)S(6)} %select_n.87), kind=kOutput, calls=%fused_computation.18.clone.1 | convolution fusion | flops 134217728 | bytes 4718596 | tf_op jit(solution)/shard_map/while/body/eval_jaxpr/dot_general | solution.py:569
  68.6 6.4 %fusion.96 = (f32[1024]{0:T(1024)S(1)}, f32[1024,1024]{0,1:T(8,128)}) fusion(f32[1024,1024]{1,0:T(8,128)} %fusion.93, bf16[1024,512]{1,0:T(8,128)(2,1)} %get-tuple-element.382, bf16[2048,512]{1,0:T(8,128)(2,1)} %get-tuple-element.381, s32[]{:T(128)S(6)} %select_n.87, s32[1024]{0:T(1024)S(1)} %eq.243, s32[1024]{0:T(1024)S(1)} %fusion.95, ...), kind=kOutput, calls=%fused_computation.115.clone.1 | convolution fusion | flops 1081080832 | bytes 10506244 | tf_op jit(solution)/shard_map/while/body/eval_jaxpr/dot_general | solution.py:564
  75.0 3.1 %fusion.97 = f32[1024]{0:T(1024)S(1)} fusion(f32[1024,1024]{0,1:T(8,128)} %get-tuple-element.343, f32[1024]{0:T(1024)S(1)} %select_maximum_fusion.2, s32[1024]{0:T(1024)S(1)} %eq.243, s32[1024]{0:T(1024)S(1)} %le.162, s32[1024]{0:T(1024)S(1)} %fusion.95, s32[1024]{0:T(1024)S(1)} %iota_add_fusion.4), kind=kLoop, calls=%fused_computation.6.clone.1 | loop fusion | flops 6290432 | bytes 4218880 | tf_op jit(solution)/shard_map/while/body/eval_jaxpr/reduce_sum | solution.py:578
  78.4 4.9 %fusion.99 = f32[1024,512]{1,0:T(8,128)} fusion(f32[1024,512]{1,0:T(8,128)} %get-tuple-element.364, f32[1024,1024]{0,1:T(8,128)S(1)} %copy-done.1, f32[1024]{0:T(1024)S(1)} %select_maximum_fusion.2, s32[1024]{0:T(1024)S(1)} %eq.243, s32[1024]{0:T(1024)S(1)} %le.162, s32[1024]{0:T(1024)S(1)} %fusion.95, s32[1024]{0:T(1024)S(1)} %iota_add_fusion.4, ...), kind=kOutput, calls=%fused_computation.9.clone.1 | convolution fusion | flops 1081606144 | bytes 9461765 | tf_op jit(solution)/shard_map/while/body/eval_jaxpr/dot_general | solution.py:579
  83.4 2.0 fusion.34
  85.4 2.2 convolution_convert_fusion.3
  87.6 1.6 convolution_convert_fusion.1.attn_ref
  89.7 1.4 fusion.36.place_ref
  93.2 1.5 reduce-precision_convert_fusion.1
  94.7 1.4 pad_maximum_fusion.router_ref
  96.2 8.5 %copy.49 = bf16[1,2,2048,704]{3,2,1,0:T(8,128)(2,1)} copy(bf16[1,2,2048,704]{2,3,1,0:T(8,128)(2,1)} %param.32) | data formatting | bytes 11534336 | tf_op args[14]
  105.3 115.3 %shard_map.176 = bf16[128,1024]{1,0:T(8,128)(2,1)} custom-call(bf16[128,2048]{1,0:T(8,128)(2,1)} %hidden_ref.1, bf16[128,2048]{1,0:T(8,128)(2,1)} %convolution_convert_fusion.1.attn_ref, f32[2,1024]{1,0:T(2,128)} %reshape.175.gain_ref, bf16[16,64,128]{2,1,0:T(8,128)(2,1)} %fusion.45.pick_ref, bf16[16,128,64]{2,1,0:T(8,128)(2,1)} %fusion.36.place_ref, ...), custom_call_target="tpu_custom_call" | custom-call | tf_op jit(solution)/shard_map/pallas_call | solution.py:451
  220.7 4.2 %reshape.177 = bf16[128,8192]{1,0:T(8,128)(2,1)} reshape(bf16[2048,512]{1,0:T(8,128)(2,1)} %get-tuple-element.398) | data formatting | bytes 4194304 | tf_op jit(solution)/shard_map/reshape | solution.py:594
  225.3 2.0 convolution_convert_fusion
  (102 shorter events, 20.2 us)
Async XLA Ops:
  0.6 3.7 %copy-start = (bf16[2048,576]{0,1:T(8,128)(2,1)S(1)}, bf16[2048,576]{0,1:T(8,128)(2,1)}, u32[]{:S(2)}) copy-start(bf16[2048,576]{0,1:T(8,128)(2,1)} %param.25) | copy-start | bytes 7077892
  0.6 5.9 %copy-start.13 = (f32[512]{0:T(512)S(1)}, f32[512]{0:T(512)}, u32[]{:S(2)}) copy-start(f32[512]{0:T(512)} %param.26) | copy-start | bytes 6148
  0.7 6.0 %copy-start.12 = (s32[128,6]{0,1:T(8,128)S(1)}, s32[128,6]{0,1:T(8,128)}, u32[]{:S(2)}) copy-start(s32[128,6]{0,1:T(8,128)} %param.22) | copy-start | bytes 9220
  0.7 3.7 %copy-start.9 = (s32[128]{0:T(128)}, s32[128]{0:T(128)S(1)}, u32[]{:S(2)}) copy-start(s32[128]{0:T(128)S(1)} %iota_add_fusion.2) | copy-start | bytes 1540
  34.1 1.5 copy-start.2
  35.8 5.9 %copy-start.3 = (bf16[2048,16]{1,0:T(8,128)(2,1)}, bf16[2048,16]{1,0:T(8,128)(2,1)S(1)}, u32[]{:S(2)}) copy-start(bf16[2048,16]{1,0:T(8,128)(2,1)S(1)} %slice.50) | copy-start | bytes 196612
  40.4 5.4 %copy-start.7 = (bf16[8,128,512]{2,1,0:T(8,128)(2,1)S(1)}, bf16[8,128,512]{2,1,0:T(8,128)(2,1)}, u32[]{:S(2)}) copy-start(bf16[8,128,512]{2,1,0:T(8,128)(2,1)} %param.27) | copy-start | bytes 3145732
  48.0 2.7 %copy-start.14 = (s32[2]{0:T(128)S(1)}, s32[2]{0:T(128)}, u32[]{:S(2)}) copy-start(s32[2]{0:T(128)} %get-tuple-element.380) | copy-start | bytes 28 | tf_op jit(solution)/shard_map/while
  48.0 3.0 %copy-start.10 = (s32[128]{0:T(128)S(1)}, s32[128]{0:T(128)}, u32[]{:S(2)}) copy-start(s32[128]{0:T(128)} %get-tuple-element.385) | copy-start | bytes 1540 | tf_op jit(solution)/shard_map/while
  57.7 3.4 %copy-start.1 = (f32[1024,1024]{0,1:T(8,128)S(1)}, f32[1024,1024]{0,1:T(8,128)}, u32[]{:S(2)}) copy-start(f32[1024,1024]{0,1:T(8,128)} %get-tuple-element.343) | copy-start | bytes 12582916 | tf_op jit(solution)/shard_map/while
  65.4 2.6 %copy-start.14 = (s32[2]{0:T(128)S(1)}, s32[2]{0:T(128)}, u32[]{:S(2)}) copy-start(s32[2]{0:T(128)} %get-tuple-element.380) | copy-start | bytes 28 | tf_op jit(solution)/shard_map/while
  65.4 3.0 %copy-start.10 = (s32[128]{0:T(128)S(1)}, s32[128]{0:T(128)}, u32[]{:S(2)}) copy-start(s32[128]{0:T(128)} %get-tuple-element.385) | copy-start | bytes 1540 | tf_op jit(solution)/shard_map/while
  75.0 3.4 %copy-start.1 = (f32[1024,1024]{0,1:T(8,128)S(1)}, f32[1024,1024]{0,1:T(8,128)}, u32[]{:S(2)}) copy-start(f32[1024,1024]{0,1:T(8,128)} %get-tuple-element.343) | copy-start | bytes 12582916 | tf_op jit(solution)/shard_map/while
  83.4 4.2 %copy-start.5 = (bf16[1024,2048]{1,0:T(8,128)(2,1)S(1)}, bf16[1024,2048]{1,0:T(8,128)(2,1)}, u32[]{:S(2)}) copy-start(bf16[1024,2048]{1,0:T(8,128)(2,1)} %param.29) | copy-start | bytes 12582916
  85.3 3.8 %copy-start.4 = (bf16[2048,16]{1,0:T(8,128)(2,1)S(1)}, bf16[2048,16]{1,0:T(8,128)(2,1)}, u32[]{:S(2)}) copy-start(bf16[2048,16]{1,0:T(8,128)(2,1)} %copy-done.3) | copy-start | bytes 196612
  87.6 4.3 %copy-start.8 = (f32[2048,16]{0,1:T(8,128)S(1)}, f32[2048,16]{0,1:T(8,128)}, u32[]{:S(2)}) copy-start(f32[2048,16]{0,1:T(8,128)} %param.31) | copy-start | bytes 393220
  96.2 8.5 %copy-start.11 = (f32[2048]{0:T(1024)S(1)}, f32[2048]{0:T(1024)}, u32[]{:S(2)}) copy-start(f32[2048]{0:T(1024)} %param.30) | copy-start | bytes 24580
  220.6 4.3 %copy-start.15 = (s32[128]{0:T(128)S(1)}, s32[128]{0:T(128)}, u32[]{:S(2)}) copy-start(s32[128]{0:T(128)} %param.23) | copy-start | bytes 1540
  220.7 8.5 %copy-start.6 = (bf16[128,1024]{1,0:T(8,128)(2,1)S(1)}, bf16[128,1024]{1,0:T(8,128)(2,1)}, u32[]{:S(2)}) copy-start(bf16[128,1024]{1,0:T(8,128)(2,1)} %shard_map.176) | copy-start | bytes 786436

commit v2 on v1

--- a/solution.py
+++ b/solution.py
@@ -112,12 +112,13 @@
 
 
 class Spread:
-    def __init__(self, buf, s, h, nz, sems):
+    def __init__(self, buf, s, h, nz, sems, blocks_first=False):
+        self.blocks_first = blocks_first
         self.buf, self.s, self.h, self.nz = buf, s, h, nz
         self.sems = sems
 
     def move(self, block, kind, index, device):
-        view = self.buf.at[self.h, block]
+        view = self.buf.at[block, self.h] if self.blocks_first else self.buf.at[self.h, block]
         return pltpu.make_async_remote_copy(
             src_ref=view,
             dst_ref=view,
@@ -147,7 +148,8 @@
     def sibling(self, back, mine):
         half = self.h if mine else 1 - self.h
         line = lax.rem(lax.div(self.s, 4) - back + self.nz, self.nz)
-        view = self.buf.at[half, pl.ds(line * 4, 4)]
+        four = pl.ds(line * 4, 4)
+        view = self.buf.at[four, half] if self.blocks_first else self.buf.at[half, four]
         return pltpu.make_async_remote_copy(
             src_ref=view,
             dst_ref=view,
@@ -190,10 +192,9 @@
 
 def gather_kernel(nz, rows_ref, out_ref, *sems):
     s, h = lax.axis_index("seq"), lax.axis_index("head")
-    half = rows_ref.shape[1]
-    out_ref[h, s] = rows_ref[h]
+    out_ref[s, h] = rows_ref[h]
     meet(s, h, nz)
-    spread = Spread(out_ref, s, h, nz, sems)
+    spread = Spread(out_ref, s, h, nz, sems, True)
     spread.send_all()
     for back in range(nz):
         spread.pass_on(back)
@@ -207,7 +208,7 @@
     nz = seq_count // 4
     out = pl.pallas_call(
         functools.partial(gather_kernel, nz),
-        out_shape=jax.ShapeDtypeStruct((2, seq_count, tok_rows // 2, width), rows.dtype),
+        out_shape=jax.ShapeDtypeStruct((seq_count, 2, tok_rows // 2, width), rows.dtype),
         in_specs=[pl.BlockSpec(memory_space=pltpu.VMEM)],
         out_specs=pl.BlockSpec(memory_space=pltpu.VMEM),
         scratch_shapes=spread_sems(nz),
@@ -215,7 +216,7 @@
             collective_id=0, has_side_effects=True, vmem_limit_bytes=16 * 1024 * 1024
         ),
     )(rows.reshape(2, tok_rows // 2, width))
-    return jnp.swapaxes(out, 0, 1).reshape(seq_count * tok_rows, width)
+    return out.reshape(seq_count * tok_rows, width)
 
 
 def expert_kernel(
@@ -347,8 +348,9 @@
         own = jnp.sum(own, axis=1, keepdims=True)
         every = jnp.sum(chosen, axis=1, keepdims=True)
         weight = ROUTE_SCALE * own / jnp.where(every > 0.0, every, 1.0)
-        gate = jnp.dot(rows, gate_up[0], preferred_element_type=jnp.float32)
-        up = jnp.dot(rows, gate_up[1], preferred_element_type=jnp.float32)
+        across = (((1,), (1,)), ((), ()))
+        gate = lax.dot_general(rows, gate_up[0], across, preferred_element_type=jnp.float32)
+        up = lax.dot_general(rows, gate_up[1], across, preferred_element_type=jnp.float32)
         act_buf[...] = (gate / (1.0 + jnp.exp(-gate)) * up * weight).astype(jnp.bfloat16)
         res_buf[...] = jnp.dot(
             act_buf[...], down[...], preferred_element_type=jnp.float32
@@ -485,6 +487,109 @@
     )(hidden, attn_part, ffn_gain.reshape(2, half), pick, place, chosen, router3, gate_up, down)
 
 
+def attend_kernel(
+    key_tile,
+    span_ref,
+    first_ref,
+    nope_ref,
+    rope_ref,
+    keys_ref,
+    key_up_ref,
+    value_up_ref,
+    out_proj_ref,
+    out_ref,
+    query,
+    acc,
+    peak,
+    total,
+    heads_buf,
+):
+    heads, tok_rows = nope_ref.shape[0], nope_ref.shape[1]
+    group = 4
+    group_rows = group * tok_rows
+    score_scale = 1.0 / math.sqrt(NOPE + ROPE)
+    contract = (((1,), (1,)), ((), ()))
+    for head in range(heads):
+        here = slice(head * tok_rows, (head + 1) * tok_rows)
+        query[here, :KV_RANK] = jnp.dot(
+            nope_ref[head], key_up_ref[head], preferred_element_type=jnp.float32
+        ).astype(jnp.bfloat16)
+        query[here, KV_RANK:] = rope_ref[head]
+    first = jnp.concatenate([first_ref[...]] * group, axis=0)
+    own = span_ref[2] + lax.broadcasted_iota(jnp.int32, (tok_rows, 1), 0)
+    own = jnp.concatenate([own] * group, axis=0)
+
+    @pl.loop(0, heads // group)
+    def _(part_no):
+        base = pl.multiple_of(part_no * group_rows, group_rows)
+        here = pl.ds(base, group_rows)
+        peak[...] = jnp.full_like(peak, MASKED)
+        total[...] = jnp.zeros_like(total)
+        acc[...] = jnp.zeros_like(acc)
+
+        @pl.loop(span_ref[0], span_ref[1])
+        def _(tile):
+            start = pl.multiple_of(tile * key_tile, key_tile)
+            keys = keys_ref[pl.ds(start, key_tile), :]
+            scores = score_scale * lax.dot_general(
+                query[here, :], keys, contract, preferred_element_type=jnp.float32
+            )
+            index = start + lax.broadcasted_iota(jnp.int32, scores.shape, 1)
+            allowed = (index <= own) & (index >= first)
+            scores = jnp.where(allowed, scores, MASKED)
+            old = peak[:, :1]
+            new = jnp.maximum(old, jnp.max(scores, axis=1, keepdims=True))
+            terms = jnp.where(allowed, jnp.exp(scores - new), 0.0)
+            fade = jnp.exp(old - new)
+            total[:, :1] = total[:, :1] * fade + jnp.sum(terms, axis=1, keepdims=True)
+            peak[:, :1] = new
+            acc[...] = acc[...] * fade + jnp.dot(
+                terms.astype(jnp.bfloat16), keys[:, :KV_RANK], preferred_element_type=jnp.float32
+            )
+
+        attended = (acc[...] / total[:, :1]).astype(jnp.bfloat16)
+        for member in range(group):
+            heads_buf[part_no * group + member] = jnp.dot(
+                attended[member * tok_rows : (member + 1) * tok_rows],
+                value_up_ref[part_no * group + member],
+                preferred_element_type=jnp.float32,
+            ).astype(jnp.bfloat16)
+
+    joined = jnp.concatenate([heads_buf[head] for head in range(heads)], axis=1)
+    out_ref[...] = jnp.dot(
+        joined, out_proj_ref[...], preferred_element_type=jnp.float32
+    ).astype(out_ref.dtype)
+
+
+def attend_rows(nope, rope, keys, key_up, value_up, out_proj, first, first_token):
+    heads, tok_rows = nope.shape[0], nope.shape[1]
+    key_tile = 512 if keys.shape[0] % 512 == 0 else 128
+    width = keys.shape[1]
+    span = jnp.stack(
+        [
+            jnp.min(first) // key_tile,
+            (first_token + tok_rows + key_tile - 1) // key_tile,
+            first_token,
+        ]
+    ).astype(jnp.int32)
+    vmem = pl.BlockSpec(memory_space=pltpu.VMEM)
+    rows = 4 * tok_rows
+    return pl.pallas_call(
+        functools.partial(attend_kernel, key_tile),
+        out_shape=jax.ShapeDtypeStruct((tok_rows, out_proj.shape[1]), jnp.bfloat16),
+        in_specs=[pl.BlockSpec(memory_space=pltpu.SMEM)] + [vmem] * 7,
+        out_specs=vmem,
+        scratch_shapes=[
+            pltpu.VMEM((heads * tok_rows, width), jnp.bfloat16),
+            pltpu.VMEM((rows, KV_RANK), jnp.float32),
+            pltpu.VMEM((rows, 128), jnp.float32),
+            pltpu.VMEM((rows, 128), jnp.float32),
+            pltpu.VMEM((heads, tok_rows, V_HEAD), jnp.bfloat16),
+        ],
+        compiler_params=pltpu.CompilerParams(vmem_limit_bytes=40 * 1024 * 1024),
+    )(span, first[:, None], nope, rope, keys, key_up, value_up, out_proj)
+
+
 def body(
     hidden,
     queries,
@@ -544,9 +649,43 @@
         payload = jnp.concatenate([latent, key_rope, route_mask.astype(jnp.bfloat16)], axis=1)
         payload = jnp.pad(payload, ((0, 0), (0, -payload.shape[1] % 128)))
         gathered = gather_rows(payload, seq_count)
-        piece_latent = gathered[:, :KV_RANK]
-        piece_rope = gathered[:, KV_RANK : KV_RANK + ROPE]
         all_masks = gathered[:, KV_RANK + ROPE : KV_RANK + ROPE + expert_count]
+        by_head = jnp.swapaxes(head_view, 0, 1)
+        rope_pad = gathered.shape[1] - KV_RANK - ROPE
+        by_head_rope = jnp.pad(jnp.swapaxes(query_rope, 0, 1), ((0, 0), (0, 0), (0, rope_pad)))
+        req_ends = running(req_len)
+        member = my_request[:, None] == jnp.arange(req_len.shape[0])[None, :]
+        first = jnp.sum(jnp.where(member, (req_ends - req_len)[None, :], 0), axis=1)
+        attn_part = attend_rows(
+            by_head[:, :, :NOPE],
+            by_head_rope,
+            gathered,
+            key_up,
+            value_up,
+            out_proj,
+            first,
+            seq_place * tok_rows,
+        )
+        source_row = source_block[:, None] * BLOCK + jnp.arange(BLOCK, dtype=jnp.int32)[None, :]
+        pick_rows = source_row[:, :, None] == jnp.arange(gathered.shape[0], dtype=jnp.int32)
+        pick_rows = (pick_rows & slot_filled[:, None, None]).reshape(DEC_SLOTS * BLOCK, -1)
+        slot_rows = jnp.dot(
+            pick_rows.astype(jnp.bfloat16), gathered, preferred_element_type=jnp.float32
+        ).astype(jnp.bfloat16)
+        decode_latent = slot_rows[:, :KV_RANK].reshape(DEC_SLOTS, BLOCK, KV_RANK)
+        decode_rope = slot_rows[:, KV_RANK : KV_RANK + ROPE].reshape(DEC_SLOTS, BLOCK * ROPE)
+        output = expert_layer(
+            hidden,
+            attn_part,
+            all_masks.reshape(seq_count, tok_rows, expert_count),
+            ffn_gain,
+            router,
+            jnp.swapaxes(expert_gate_up[0], 1, 2),
+            expert_down[0],
+            seq_place,
+            seq_count,
+        )
+        return (output, decode_latent, decode_rope)
     else:
         piece_latent = lax.all_gather(latent, "seq", axis=0, tiled=True)
         piece_rope = lax.all_gather(key_rope, "seq", axis=0, tiled=True)
@@ -617,19 +756,6 @@
     )
     decode_latent = slot_latent.astype(jnp.bfloat16).reshape(DEC_SLOTS, BLOCK, KV_RANK)
     decode_rope = slot_rope.astype(jnp.bfloat16)
-    if fast:
-        output = expert_layer(
-            hidden,
-            attn_part.astype(jnp.bfloat16),
-            all_masks.reshape(seq_count, tok_rows, expert_count),
-            ffn_gain,
-            router,
-            expert_gate_up[0],
-            expert_down[0],
-            seq_place,
-            seq_count,
-        )
-        return (output, decode_latent, decode_rope)
     mixed_rows = hidden.astype(jnp.float32) + lax.psum(
         attn_part.astype(jnp.bfloat16), "head"
     ).astype(jnp.float32)

time: 231 us -> 187 us (0.81)
  matrix products: 37.5 us -> 3.74 us
  local copies, waits for them, and re-layouts: 29.2 us -> 11.5 us
  Pallas kernels: 142 us -> 154 us
  other arithmetic: 20 us -> 14.4 us
  between operations: 0.93 us -> 3.51 us
    dot_general x11 -> x1, matrix products: 34.4 us -> 0.62 us  [body(): jnp.dot(pick_rows.astype(jnp.bfloat16), gathered, preferred_element_type=...]
    unnamed x32 -> x22, local copies, waits for them, and re-layouts: 14.2 us -> 4.17 us
    reduce_sum x2 -> x0, other arithmetic: 6.19 us -> none  [key_block(): total_now = total_now * fade_factor + jnp.sum(exp_terms, axis=1)]
    pallas_call x1, Pallas kernels: 115 us -> 121 us  [expert_layer(): pl.pallas_call(functools.partial(expert_kernel, nz), out_shape=jax.ShapeD...]
    pallas_call x0 -> x1, Pallas kernels: none -> 5.65 us  [attend_rows(): pl.pallas_call(functools.partial(attend_kernel, key_tile), out_shape=jax....]
    slice x2 -> x3, local copies, waits for them, and re-layouts: 4.15 us -> 0.68 us  [the longest x1 0.63 us: body(): decode_latent = slot_rows[:, :KV_RANK].reshape(DEC_SLOTS, BLOCK, KV_RANK)]
    reshape x2, local copies, waits for them, and re-layouts: 4.59 us -> 1.88 us  [the longest x1 1.2 us: body(): head_view = queries.reshape(tok_rows, heads_here, NOPE + ROPE)]
where the time goes in v2:
time: 187 us
  Pallas kernels  154 us (82%)
  other arithmetic  14.4 us (8%)
  local copies, waits for them, and re-layouts  11.5 us (6%)
  matrix products  3.74 us (2%)
  between operations  3.51 us (2%)
    pallas_call x1, Pallas kernels, expert_layer(): pl.pallas_call(functools.partial(expert_kernel, nz), out_shape=jax.ShapeD...  121 us
    pallas_call x1, Pallas kernels, gather_rows(): pl.pallas_call(functools.partial(gather_kernel, nz), out_shape=jax.ShapeD...  26.8 us
    pallas_call x1, Pallas kernels, attend_rows(): pl.pallas_call(functools.partial(attend_kernel, key_tile), out_shape=jax....  5.65 us
    unnamed x22, local copies, waits for them, and re-layouts  4.17 us

profile of v2, /device:TPU:0, one launch (start us, length us, event | category | flops | bytes accessed | tf_op | source)
XLA Modules:
  0.0 187.1 jit_solution(16101761353485887355)
XLA Ops:
  0.7 0.9 fusion.27
  2.3 0.8 compare_reduce_fusion.1
  3.1 0.8 fusion.26
  4.1 1.2 fusion
  5.5 0.8 select_reduce_fusion
  9.7 0.7 fusion.25
  10.4 1.3 reshape.164.gain_ref
  11.8 1.9 %fusion.10 = f32[128,576]{0,1:T(8,128)S(1)} fusion(bf16[2048,576]{0,1:T(8,128)(2,1)S(1)} %copy-done, bf16[128,2048]{1,0:T(8,128)(2,1)} %hidden_ref.1, f32[2048]{0:T(1024)} %param.22, f32[128]{0:T(128)S(1)} %add_rsqrt_fusion.1), kind=kOutput, calls=%fused_computation.23 | convolution fusion | flops 303038464 | bytes 3187200 | tf_op jit(solution)/shard_map/dot_general | solution.py:637
  14.3 0.7 copy.49
  15.1 0.7 copy.46
  16.1 0.7 copy-done.5
  16.8 1.2 copy.45
  18.1 1.0 copy.47
  19.1 1.4 fusion.7
  20.7 1.3 copy.53
  22.0 1.6 reduce-precision_convert_fusion.1
  23.6 1.4 pad_maximum_fusion.router_ref
  25.0 26.8 %shard_map.175 = bf16[16,2,64,640]{3,2,1,0:T(8,128)(2,1)S(1)} custom-call(bf16[2,64,640]{2,1,0:T(8,128)(2,1)S(1)} %bitcast.22), custom_call_target="tpu_custom_call" | custom-call | tf_op jit(solution)/shard_map/pallas_call | solution.py:209
  51.8 5.6 %shard_map.176.attn_ref = bf16[128,2048]{1,0:T(8,128)(2,1)S(1)} custom-call(s32[3]{0:T(128)S(1)} %pad_add_fusion.span_ref, s32[128,1]{1,0:T(8,128)S(1)} %copy.52.first_ref, bf16[8,128,128]{2,1,0:T(8,128)(2,1)S(1)} %slice.42.nope_ref, bf16[8,128,128]{2,1,0:T(8,128)(2,1)S(1)} %pad.16.rope_ref, bf16[2048,640]{1,0:T(8,128)(2,1)S(1)} %bitcast.19, ...), custom_call_target="tpu_custom_call" | custom-call | tf_op jit(solution)/shard_map/pallas_call | solution.py:577
  59.4 1.1 fusion.12.chosen_ref
  61.8 0.8 fusion.18.pick_ref
  62.6 1.4 fusion.5.place_ref
  64.0 121.4 %shard_map.177 = bf16[128,1024]{1,0:T(8,128)(2,1)} custom-call(bf16[128,2048]{1,0:T(8,128)(2,1)} %hidden_ref.1, bf16[128,2048]{1,0:T(8,128)(2,1)} %copy-done.2, f32[2,1024]{1,0:T(2,128)} %reshape.164.gain_ref, bf16[16,64,128]{2,1,0:T(8,128)(2,1)} %fusion.18.pick_ref, bf16[16,128,64]{2,1,0:T(8,128)(2,1)} %fusion.5.place_ref, ...), custom_call_target="tpu_custom_call" | custom-call | tf_op jit(solution)/shard_map/pallas_call | solution.py:453
  185.4 1.7 copy.56
  (53 shorter events, 6.2 us)
Async XLA Ops:
  0.6 11.2 %copy-start = (bf16[2048,576]{0,1:T(8,128)(2,1)S(1)}, bf16[2048,576]{0,1:T(8,128)(2,1)}, u32[]{:S(2)}) copy-start(bf16[2048,576]{0,1:T(8,128)(2,1)} %param.23) | copy-start | bytes 7077892
  0.6 13.3 %copy-start.8 = (f32[512]{0:T(512)S(1)}, f32[512]{0:T(512)}, u32[]{:S(2)}) copy-start(f32[512]{0:T(512)} %param.24) | copy-start | bytes 6148
  5.3 10.5 %copy-start.6 = (bf16[128,1536]{1,0:T(8,128)(2,1)S(1)}, bf16[128,1536]{1,0:T(8,128)(2,1)}, u32[]{:S(2)}) copy-start(bf16[128,1536]{1,0:T(8,128)(2,1)} %param.17) | copy-start | bytes 1179652
  16.0 0.7 copy-start.5
  19.1 1.6 copy-start.7
  22.0 29.8 %copy-start.4 = (bf16[8,512,128]{2,1,0:T(8,128)(2,1)S(1)}, bf16[8,512,128]{2,1,0:T(8,128)(2,1)}, u32[]{:S(2)}) copy-start(bf16[8,512,128]{2,1,0:T(8,128)(2,1)} %value_up_ref.1) | copy-start | bytes 3145732
  23.6 28.2 %copy-start.1 = (bf16[1024,2048]{1,0:T(8,128)(2,1)S(1)}, bf16[1024,2048]{1,0:T(8,128)(2,1)}, u32[]{:S(2)}) copy-start(bf16[1024,2048]{1,0:T(8,128)(2,1)} %out_proj_ref.1) | copy-start | bytes 12582916
  23.6 28.2 %copy-start.3 = (bf16[8,128,512]{2,1,0:T(8,128)(2,1)S(1)}, bf16[8,128,512]{2,1,0:T(8,128)(2,1)}, u32[]{:S(2)}) copy-start(bf16[8,128,512]{2,1,0:T(8,128)(2,1)} %key_up_ref.1) | copy-start | bytes 3145732
  57.5 3.0 %copy-start.2 = (bf16[128,2048]{1,0:T(8,128)(2,1)}, bf16[128,2048]{1,0:T(8,128)(2,1)S(1)}, u32[]{:S(2)}) copy-start(bf16[128,2048]{1,0:T(8,128)(2,1)S(1)} %shard_map.176.attn_ref) | copy-start | bytes 1572868

commit v3 on v2

--- a/solution.py
+++ b/solution.py
@@ -259,7 +259,7 @@
     s, h = lax.axis_index("seq"), lax.axis_index("head")
     cols = hidden_ref.shape[1]
     half = cols // 2
-    slots = pick_ref.shape[1]
+    slots = pick_ref.shape[1] // 2
     loads = [
         pltpu.make_async_copy(gate_up_hbm, gate_up, load_sem.at[0]),
         pltpu.make_async_copy(down_hbm, down, load_sem.at[1]),
@@ -332,12 +332,13 @@
     def feed(back):
         spread.sibling(back, False).wait_recv()
         base = line_of(back) * 4
-        for c in range(4):
-            pick = pick_ref[base + c]
+        for c in range(2):
+            pick = pick_ref[line_of(back) * 2 + c]
             for side in range(2):
-                rows_buf[c * slots : (c + 1) * slots, side * half : (side + 1) * half] = jnp.dot(
-                    pick, x_buf[side, base + c], preferred_element_type=jnp.float32
-                ).astype(jnp.bfloat16)
+                pair = x_buf[side, pl.ds(base + 2 * c, 2)].reshape(pick.shape[1], half)
+                rows_buf[2 * c * slots : 2 * (c + 1) * slots, side * half : (side + 1) * half] = (
+                    jnp.dot(pick, pair, preferred_element_type=jnp.float32).astype(jnp.bfloat16)
+                )
         rows = rows_buf[...]
         logit = jnp.dot(rows, router_ref[...], preferred_element_type=jnp.float32)
         width = logit.shape[1] // 3
@@ -355,13 +356,14 @@
         res_buf[...] = jnp.dot(
             act_buf[...], down[...], preferred_element_type=jnp.float32
         ).astype(jnp.bfloat16)
-        for c in range(4):
-            for side in range(2):
-                part[side, base + c] = jnp.dot(
-                    place_ref[base + c],
-                    res_buf[c * slots : (c + 1) * slots, side * half : (side + 1) * half],
+        for side in range(2):
+            for c in range(2):
+                pair = jnp.dot(
+                    place_ref[line_of(back) * 2 + c],
+                    res_buf[2 * c * slots : 2 * (c + 1) * slots, side * half : (side + 1) * half],
                     preferred_element_type=jnp.float32,
                 ).astype(jnp.bfloat16)
+                part[side, pl.ds(base + 2 * c, 2)] = pair.reshape(2, -1, half)
         give0(back).start()
 
     def fold0(back):
@@ -423,6 +425,12 @@
         give2(back).wait_send()
         if back:
             give1(back).wait_send()
+
+
+def paired(blocks):
+    count, rows, cols = blocks.shape
+    same = jnp.eye(2, dtype=blocks.dtype)[None, :, None, :, None]
+    return (blocks.reshape(count // 2, 2, rows, 1, cols) * same).reshape(-1, 2 * rows, 2 * cols)
 
 
 def expert_layer(hidden, attn_part, masks, ffn_gain, router, gate_up, down, seq_place, seq_count):
@@ -441,6 +449,8 @@
     place = place.astype(jnp.bfloat16)
     wide_masks = jnp.pad(masks, ((0, 0), (0, 0), (0, 128 - expert_count)))
     chosen = jnp.einsum("brt,bte->bre", pick, wide_masks, preferred_element_type=jnp.float32)
+    pick = paired(pick)
+    place = paired(place)
     router = jnp.pad(router, ((0, 0), (0, 128 - expert_count)))
     high = lax.reduce_precision(router, 8, 7)
     middle = lax.reduce_precision(router - high, 8, 7)

time: 187 us -> 192 us (1.027); the launches traced: 187 us -> 194 us
  local copies, waits for them, and re-layouts: 11.5 us -> 15.9 us
  Pallas kernels: 154 us -> 156 us
    mul x0 -> x8, local copies, waits for them, and re-layouts: none -> 3.65 us  [paired(): blocks.reshape(count // 2, 2, rows, 1, cols) * same]
    pallas_call x1, Pallas kernels: 121 us -> 124 us  [expert_layer(): pl.pallas_call(functools.partial(expert_kernel, nz), out_shape=jax.ShapeD...]
    unnamed x22 -> x28, local copies, waits for them, and re-layouts: 4.17 us -> 4.82 us
where the time goes in v3:
time: 192 us; the launch traced here: 194 us
  Pallas kernels  156 us (81%)
  local copies, waits for them, and re-layouts  15.9 us (8%)
  other arithmetic  15 us (8%)
  matrix products  3.72 us (2%)
  between operations  3.6 us (2%)
    pallas_call x1, Pallas kernels, expert_layer(): pl.pallas_call(functools.partial(expert_kernel, nz), out_shape=jax.ShapeD...  124 us
    pallas_call x1, Pallas kernels, gather_rows(): pl.pallas_call(functools.partial(gather_kernel, nz), out_shape=jax.ShapeD...  26.8 us
    pallas_call x1, Pallas kernels, attend_rows(): pl.pallas_call(functools.partial(attend_kernel, key_tile), out_shape=jax....  5.64 us
    unnamed x28, local copies, waits for them, and re-layouts  4.82 us

profile of v3, /device:TPU:0, one launch (start us, length us, event | category | flops | bytes accessed | tf_op | source)
XLA Modules:
  0.0 194.4 jit_solution(16216797104373471985)
XLA Ops:
  0.7 0.9 fusion.26
  2.4 0.8 compare_reduce_fusion.1
  3.2 0.8 fusion.25
  4.2 1.2 fusion
  5.6 0.7 select_reduce_fusion
  10.5 1.3 reshape.201.gain_ref
  13.5 1.9 fusion.8
  16.0 0.7 copy.55
  17.7 0.7 copy-done.5
  18.5 1.2 copy.51
  19.7 1.0 copy.53
  20.7 1.4 fusion.5
  22.3 1.3 copy.62
  23.7 1.6 reduce-precision_convert_fusion.1
  25.3 1.4 pad_maximum_fusion.router_ref
  26.6 26.8 %shard_map.175 = bf16[16,2,64,640]{3,2,1,0:T(8,128)(2,1)S(1)} custom-call(bf16[2,64,640]{2,1,0:T(8,128)(2,1)S(1)} %bitcast.37), custom_call_target="tpu_custom_call" | custom-call | tf_op jit(solution)/shard_map/pallas_call | solution.py:209
  53.5 5.6 %shard_map.176.attn_ref = bf16[128,2048]{1,0:T(8,128)(2,1)S(1)} custom-call(s32[3]{0:T(128)S(1)} %pad_add_fusion.span_ref, s32[128,1]{1,0:T(8,128)S(1)} %copy.58.first_ref, bf16[8,128,128]{2,1,0:T(8,128)(2,1)S(1)} %slice.42.nope_ref, bf16[8,128,128]{2,1,0:T(8,128)(2,1)S(1)} %pad.16.rope_ref, bf16[2048,640]{1,0:T(8,128)(2,1)S(1)} %bitcast.34, ...), custom_call_target="tpu_custom_call" | custom-call | tf_op jit(solution)/shard_map/pallas_call | solution.py:587
  61.1 1.1 fusion.10.chosen_ref
  63.5 1.0 and_convert_fusion
  65.4 0.9 broadcast_multiply_fusion.1.pick_ref
  66.3 1.3 mul.200
  68.3 0.8 broadcast_multiply_fusion.place_ref
  69.1 123.6 %shard_map.177 = bf16[128,1024]{1,0:T(8,128)(2,1)} custom-call(bf16[128,2048]{1,0:T(8,128)(2,1)} %hidden_ref.1, bf16[128,2048]{1,0:T(8,128)(2,1)} %copy-done.2, f32[2,1024]{1,0:T(2,128)} %reshape.201.gain_ref, bf16[8,128,256]{2,1,0:T(8,128)(2,1)} %broadcast_multiply_fusion.1.pick_ref, bf16[8,256,128]{2,1,0:T(8,128)(2,1)} %broadcast_multiply_fusion.place_ref, ...), custom_call_target="tpu_custom_call" | custom-call | tf_op jit(solution)/shard_map/pallas_call | solution.py:463
  192.7 1.7 copy.71
  (72 shorter events, 10.8 us)
Async XLA Ops:
  0.6 12.9 %copy-start = (bf16[2048,576]{0,1:T(8,128)(2,1)S(1)}, bf16[2048,576]{0,1:T(8,128)(2,1)}, u32[]{:S(2)}) copy-start(bf16[2048,576]{0,1:T(8,128)(2,1)} %param.23) | copy-start | bytes 7077892
  0.6 15.0 %copy-start.10 = (f32[512]{0:T(512)S(1)}, f32[512]{0:T(512)}, u32[]{:S(2)}) copy-start(f32[512]{0:T(512)} %param.24) | copy-start | bytes 6148
  12.8 4.7 %copy-start.6 = (bf16[128,1536]{1,0:T(8,128)(2,1)S(1)}, bf16[128,1536]{1,0:T(8,128)(2,1)}, u32[]{:S(2)}) copy-start(bf16[128,1536]{1,0:T(8,128)(2,1)} %param.17) | copy-start | bytes 1179652
  17.7 0.7 copy-start.5
  20.7 1.6 copy-start.9
  23.7 29.8 %copy-start.4 = (bf16[8,512,128]{2,1,0:T(8,128)(2,1)S(1)}, bf16[8,512,128]{2,1,0:T(8,128)(2,1)}, u32[]{:S(2)}) copy-start(bf16[8,512,128]{2,1,0:T(8,128)(2,1)} %value_up_ref.1) | copy-start | bytes 3145732
  25.3 28.2 %copy-start.1 = (bf16[1024,2048]{1,0:T(8,128)(2,1)S(1)}, bf16[1024,2048]{1,0:T(8,128)(2,1)}, u32[]{:S(2)}) copy-start(bf16[1024,2048]{1,0:T(8,128)(2,1)} %out_proj_ref.1) | copy-start | bytes 12582916
  25.3 28.2 %copy-start.3 = (bf16[8,128,512]{2,1,0:T(8,128)(2,1)S(1)}, bf16[8,128,512]{2,1,0:T(8,128)(2,1)}, u32[]{:S(2)}) copy-start(bf16[8,128,512]{2,1,0:T(8,128)(2,1)} %key_up_ref.1) | copy-start | bytes 3145732
  59.2 0.8 copy-start.2
  60.0 5.4 %copy-start.8 = (bf16[16,8,2,128]{3,1,2,0:T(8,128)(2,1)S(1)}, bf16[16,8,2,128]{3,1,2,0:T(8,128)(2,1)}, u32[]{:S(2)}) copy-start(bf16[16,8,2,128]{3,1,2,0:T(8,128)(2,1)} %copy.69) | copy-start | bytes 196612
  65.1 3.2 %copy-start.7 = (bf16[256,128]{1,0:T(8,128)(2,1)S(1)}, bf16[256,128]{1,0:T(8,128)(2,1)}, u32[]{:S(2)}) copy-start(bf16[256,128]{1,0:T(8,128)(2,1)} %copy.60) | copy-start | bytes 196612
